TPU v7x, 32 devices: a whole 2x2x4 slice. The times are simulated.
32 devices in a mesh: groups: 2 (over x), expert: 16 (over z, y, core).
Axes of the slice: x: 2, y: 2, z: 4, core: 2. Of those that a mesh axis runs over, the one named last changes fastest.
Arguments:
- tokens: bfloat16 [384, 3584], P(('groups', 'expert')), parts along dimension 0, may hold values from -6 to 6
- expert_ids: int32 [384, 8], P(('groups', 'expert')), parts along dimension 0, may hold values from 0 to 15, all different within a row; in each aligned block of 12 rows (0 to 11, 12 to 23, ...) at most 8 rows name the same one
- gate_weights: float32 [384, 8], P(('groups', 'expert')), parts along dimension 0, may hold values from 0.1 to 1
- w_gate: bfloat16 [16, 3584, 2048], P('expert'), may hold values from -0.09375 to 0.09375
- w_up: bfloat16 [16, 3584, 2048], P('expert'), may hold values from -0.09375 to 0.09375
- w_down: bfloat16 [16, 2048, 3584], P('expert'), may hold values from -0.125 to 0.125
Outputs:
- moe_out: bfloat16 [384, 3584], P(('groups', 'expert')), parts along dimension 0
There are 2 independent parts, one for each index of `groups`. A program takes and returns all parts, laid end to end along the dimension named above; an argument that names none is the same for every part. Nothing has to cross between parts.
Inputs may be any that keep to these rules, and one draw needn't show every extreme that they name: `expert_ids`: each row names 8 different experts. Within the rows of one block (one device's 12 tokens) no expert is named more than 8 times, and in every draw some expert is named exactly 8 times in some block.
All inputs are finite; a program needn't handle non-finite values.
Results may differ from a plain program's by a relative error of at most 0.005.
Values may be sent and summed in bfloat16 or wider, within the bound.
No kernel may reach another device: no remote copies, remote signals or barrier semaphores. Data moves between devices by JAX's collectives and lax.ppermute only.
A program may use at most 128 MiB of HBM per device.

v0:
```python
import functools

import jax
import jax.numpy as jnp
from jax import lax
from jax.experimental import pallas as pl
from jax.experimental.pallas import tpu as pltpu
from jax.sharding import PartitionSpec as P

EXPERTS = 16
CAP = 8
LANES = 128
CHUNKS = 2
MIB = 1024 * 1024
BF16 = jnp.bfloat16
F32 = jnp.float32
IN_VMEM = pl.BlockSpec(memory_space=pltpu.VMEM)
ANYWHERE = pl.BlockSpec(memory_space=pl.ANY)


def iota(shape, dim):
    return lax.broadcasted_iota(jnp.int32, shape, dim)


def near(x):
    return pltpu.with_memory_space_constraint(x, pltpu.VMEM)


def far(x):
    return pltpu.with_memory_space_constraint(x, pltpu.HBM)


def pack_kernel(tokens_ref, ids_ref, weights_ref, out_ref):
    rows, width = tokens_ref.shape
    half = width // 2
    ids = ids_ref[...].T
    weights = weights_ref[...].T
    expert_of = lax.rem(iota((rows, LANES), 1), EXPERTS)
    kind = lax.div(iota((rows, LANES), 1), EXPERTS)
    chosen = jnp.zeros((rows, LANES), F32)
    weight = jnp.zeros((rows, LANES), F32)
    for j in range(ids.shape[1]):
        same = ids[:, j : j + 1] == expert_of
        chosen = chosen + jnp.where(same, 1.0, 0.0)
        weight = weight + jnp.where(same, weights[:, j : j + 1], 0.0)
    rank = jnp.zeros((rows, LANES), F32)
    row_of = iota((rows, LANES), 0)
    for r in range(rows - 1):
        rank = rank + jnp.where(row_of > r, chosen[r : r + 1, :], 0.0)
    high = weight.astype(BF16).astype(F32)
    middle = (weight - high).astype(BF16).astype(F32)
    low = weight - high - middle
    routing = jnp.where(
        kind == 0,
        chosen * (rank + 1.0),
        jnp.where(kind == 1, high, jnp.where(kind == 2, middle, jnp.where(kind == 3, low, 0.0))),
    )
    tokens = tokens_ref[...].astype(F32)
    out_ref[:, :half] = jnp.concatenate([tokens[:, :half], tokens[:, half:]], axis=0).astype(BF16)
    out_ref[:, half:] = jnp.concatenate([routing, routing], axis=0).astype(BF16)


def load_kernel(spans, w_ref, *refs):
    out_ref, sems = refs[-2:]
    copies, at = [], 0
    for i, (begin, size) in enumerate(spans):
        copies.append(
            pltpu.make_async_copy(w_ref.at[:, pl.ds(begin, size)], out_ref.at[:, pl.ds(at, size)], sems.at[i])
        )
        at += size
    for copy in copies:
        copy.start()
    for copy in copies:
        copy.wait()


def load(w, spans, *after):
    size = sum(s for _, s in spans)
    return pl.pallas_call(
        functools.partial(load_kernel, spans),
        out_shape=pltpu.VMEM((w.shape[0], size), w.dtype),
        in_specs=[ANYWHERE] * (1 + len(after)),
        out_specs=IN_VMEM,
        scratch_shapes=[pltpu.SemaphoreType.DMA((len(spans),))],
        compiler_params=pltpu.CompilerParams(vmem_limit_bytes=MIB),
        cost_estimate=pl.CostEstimate(flops=0, bytes_accessed=4 * w.shape[0] * size, transcendentals=0),
        name="load",
    )(far(w), *after)


def project(hidden, down, weight, back, keep_ref, send_ref):
    span = keep_ref.shape[1]
    act = jnp.dot(hidden, down[...], preferred_element_type=F32)
    act = (act * weight).astype(BF16)
    both = jnp.concatenate([act[:, :span], act[:, span:]], axis=0)
    spread = jnp.dot(back, both, preferred_element_type=F32).astype(BF16)
    keep_ref[...] = spread[: keep_ref.shape[0]]
    send_ref[...] = spread[keep_ref.shape[0] :]


def expert_kernel(rows, planes, gates, spans, *refs):
    plane_refs, refs = refs[:planes], refs[planes:]
    gate_refs, up_refs, down_hbm, refs = refs[:gates], refs[gates : 2 * gates], refs[2 * gates], refs[2 * gates + 1 :]
    keep_ref, send_ref, hidden, weight_ref, back_ref, later_refs, x, down, sems = (*refs[:5], refs[5:-3], *refs[-3:])
    half = x.shape[1] // 2
    slots = x.shape[0]
    copies = []
    for i, (begin, size) in enumerate(spans):
        target = (down, *later_refs)[i // 2].at[:, pl.ds(i % 2 * size, size)]
        copies.append(pltpu.make_async_copy(down_hbm.at[:, pl.ds(begin, size)], target, sems.at[i]))
    for copy in copies:
        copy.start()

    expert = lax.rem(lax.axis_index("expert"), EXPERTS)
    pick_row = jnp.where(iota((slots, LANES), 1) == expert, 1.0, 0.0).astype(BF16)
    pick_col = jnp.where(iota((LANES, slots), 0) == expert, 1.0, 0.0).astype(BF16)

    def table(rank, packed_dim, slot_dim, first):
        at = iota(rank.shape, packed_dim) + first
        block = lax.div(at, 2 * rows)
        second = (at - block * (2 * rows)) >= rows
        hit = (rank > 0) & (iota(rank.shape, slot_dim) == block * CAP + rank.astype(jnp.int32) - 1)
        one = jnp.where(hit, 1.0, 0.0)
        return (jnp.where(second, 0.0, one).astype(BF16), jnp.where(second, one, 0.0).astype(BF16))

    first, left_x, right_x, slot_routing = 0, 0.0, 0.0, 0.0
    for ref in plane_refs:
        count = ref.shape[0]
        routing = ref[:, half:]
        rank_row = lax.dot_general(pick_row, routing, (((1,), (1,)), ((), ())), preferred_element_type=F32)
        rank_col = jnp.dot(routing, pick_col, preferred_element_type=F32)
        left, right = table(rank_row, 1, 0, first)
        back_left, back_right = table(rank_col, 0, 1, first)
        back_ref[first : first + count, :slots] = back_left
        back_ref[first : first + count, slots:] = back_right
        left_x = left_x + jnp.dot(left, ref[:, :half], preferred_element_type=F32)
        right_x = right_x + jnp.dot(right, ref[:, :half], preferred_element_type=F32)
        slot_routing = slot_routing + jnp.dot(left, routing, preferred_element_type=F32)
        first += count
    x[:, :half] = left_x.astype(BF16)
    x[:, half:] = right_x.astype(BF16)
    lane = iota(slot_routing.shape, 1)
    is_weight = (lax.rem(lane, EXPERTS) == expert) & (lane >= EXPERTS) & (lane < 4 * EXPERTS)
    weight = jnp.sum(jnp.where(is_weight, slot_routing, 0.0), axis=1, keepdims=True)
    weight_ref[...] = jnp.broadcast_to(weight, weight_ref.shape)

    at = 0
    for gate_ref, up_ref in zip(gate_refs, up_refs):
        units = gate_ref.shape[1]
        tile = 512 if units % 512 == 0 else units
        for i in range(units // tile):
            cols = slice(i * tile, (i + 1) * tile)
            gate_act = jnp.dot(x[...], gate_ref[:, cols], preferred_element_type=F32)
            up_act = jnp.dot(x[...], up_ref[:, cols], preferred_element_type=F32)
            hidden[:, at : at + tile] = (gate_act / (1.0 + jnp.exp(-gate_act)) * up_act).astype(BF16)
            at += tile
    for copy in copies[:2]:
        copy.wait()
    project(hidden[...], down, weight, back_ref[...], keep_ref, send_ref)
    for copy in copies[2:]:
        copy.wait()


def project_kernel(hidden, weight_ref, back, down, keep_ref, send_ref):
    project(hidden[...], down, weight_ref[:, :1], back[...], keep_ref, send_ref)


def body(tokens, expert_ids, gate_weights, w_gate, w_up, w_down):
    size = lax.axis_size("expert")
    steps = size // 4
    rows, width = tokens.shape
    units = w_gate.shape[2]
    half = width // 2
    block = 2 * rows
    count = size * block
    slots = size * CAP
    span = half // CHUNKS

    def send(x, pairs):
        return lax.ppermute(x, "expert", pairs)

    flip_core = [(i, i ^ 1) for i in range(size)]
    flip_second = [(i, i ^ 2) for i in range(size)]

    def shift(s):
        return [(i, (i + 4 * s) % size) for i in range(size)]

    own = pl.pallas_call(
        pack_kernel,
        out_shape=pltpu.VMEM((block, half + LANES), BF16),
        name="pack",
    )(tokens, expert_ids.T, gate_weights.T)
    low, high = [(0, units // 2)], [(units // 2, units // 2)]
    gates, ups = [load(w_gate[0], low)], [load(w_up[0], low)]
    spans = [(c * span + h * half, span) for c in range(CHUNKS) for h in range(2)]

    shifted = [send(own, shift(s)) for s in range(1, steps)]
    across = send(own, flip_second)
    column = jnp.concatenate([own] + shifted, axis=0)
    onward, gates[0], ups[0] = lax.optimization_barrier((column[block:], gates[0], ups[0]))
    plane = jnp.concatenate([column, across, send(onward, flip_second)], axis=0)
    gates.append(load(w_gate[0], high, onward))
    ups.append(load(w_up[0], high, onward))
    plane, gates[1], ups[1] = lax.optimization_barrier((plane, gates[1], ups[1]))
    other = send(plane, flip_core)

    outs = [pltpu.VMEM((count // 2, span), BF16)] * 2
    keep, away, hidden, weight, back, *downs = pl.pallas_call(
        functools.partial(expert_kernel, rows, 2, len(gates), spans),
        out_shape=outs
        + [
            pltpu.VMEM((slots, units), BF16),
            pltpu.VMEM((slots, LANES), F32),
            pltpu.VMEM((count, 2 * slots), BF16),
        ]
        + [pltpu.VMEM((units, 2 * span), BF16)] * (CHUNKS - 1),
        in_specs=[IN_VMEM] * (2 + 2 * len(gates)) + [ANYWHERE],
        out_specs=[IN_VMEM] * (4 + CHUNKS),
        scratch_shapes=[
            pltpu.VMEM((slots, width), BF16),
            pltpu.VMEM((units, 2 * span), BF16),
            pltpu.SemaphoreType.DMA((len(spans),)),
        ],
        compiler_params=pltpu.CompilerParams(vmem_limit_bytes=14 * MIB),
        cost_estimate=pl.CostEstimate(
            flops=5 * slots * width * units, bytes_accessed=4 * width * units, transcendentals=slots * units
        ),
        name="experts",
    )(near(plane), near(other), *gates, *ups, far(w_down[0]))
    results = [(keep, away)]
    for down in downs:
        results.append(
            pl.pallas_call(
                project_kernel,
                out_shape=outs,
                in_specs=[IN_VMEM] * 4,
                out_specs=[IN_VMEM] * 2,
                compiler_params=pltpu.CompilerParams(vmem_limit_bytes=14 * MIB),
                cost_estimate=pl.CostEstimate(
                    flops=slots * width * units, bytes_accessed=width * units, transcendentals=0
                ),
                name="project",
            )(hidden, weight, back, down)
        )

    def add(a, b):
        return (a.astype(F32) + b.astype(F32)).astype(BF16)

    totals = []
    for keep, away in results:
        chip = add(keep, send(away, flip_core))
        line = add(chip[: count // 4], send(chip[count // 4 :], flip_second))
        total = line[:block].astype(F32)
        for s in range(1, steps):
            total = total + send(line[s * block : (s + 1) * block], shift(steps - s)).astype(F32)
        totals.append(total.astype(BF16))
    return jnp.concatenate([t[:rows] for t in totals] + [t[rows:] for t in totals], axis=1)


def solution(mesh):
    return jax.shard_map(
        body,
        mesh=mesh,
        in_specs=(
            P(("groups", "expert"), None),
            P(("groups", "expert"), None),
            P(("groups", "expert"), None),
            P("expert", None, None),
            P("expert", None, None),
            P("expert", None, None),
        ),
        out_specs=P(("groups", "expert"), None),
        check_vma=False,
    )
```

profile of v0, /device:TPU:0, one launch (start us, length us, event | category | flops | bytes accessed | tf_op | source)
XLA Modules:
  0.0 56.3 jit_solution(15089100328904359074)
XLA Ops:
  0.0 1.1 %pack.1 = bf16[24,1920]{1,0:T(8,128)(2,1)S(1)} custom-call(bf16[12,3584]{1,0:T(8,128)(2,1)} %tokens_ref.1, s32[8,12]{1,0:T(8,128)} %bitcast.10, f32[8,12]{1,0:T(8,128)} %bitcast.11), custom_call_target="tpu_custom_call" | custom-call | tf_op jit(solution)/shard_map/pack/pallas_call | solution.py:188
  1.1 3.0 %collective-permute-start.3 = (bf16[24,1920]{1,0:T(8,128)(2,1)S(1)}, bf16[24,1920]{1,0:T(8,128)(2,1)S(1)}, u32[]{:S(2)}, u32[]{:S(2)}) collective-permute-start(bf16[24,1920]{1,0:T(8,128)(2,1)S(1)} %pack.1), channel_id=1, source_target_pairs={{0,2},{1,3},{2,0},{3,1},{4,6},{5,7},{6,4},{7,5},{8,10},{9,11},{10,... | collective-permute-start | bytes 276488 | tf_op jit(solution)/shard_map/ppermute | solution.py:180
  4.2 3.6 %collective-permute-start.2 = (bf16[24,1920]{1,0:T(8,128)(2,1)S(1)}, bf16[24,1920]{1,0:T(8,128)(2,1)S(1)}, u32[]{:S(2)}, u32[]{:S(2)}) collective-permute-start(bf16[24,1920]{1,0:T(8,128)(2,1)S(1)} %pack.1), channel_id=1, source_target_pairs={{0,12},{1,13},{2,14},{3,15},{4,0},{5,1},{6,2},{7,3},{8,4},{9,5},{1... | collective-permute-start | bytes 276488 | tf_op jit(solution)/shard_map/ppermute | solution.py:180
  7.8 1.0 %collective-permute-start = (bf16[24,1920]{1,0:T(8,128)(2,1)S(1)}, bf16[24,1920]{1,0:T(8,128)(2,1)S(1)}, u32[]{:S(2)}, u32[]{:S(2)}) collective-permute-start(bf16[24,1920]{1,0:T(8,128)(2,1)S(1)} %pack.1), channel_id=1, source_target_pairs={{0,4},{1,5},{2,6},{3,7},{4,8},{5,9},{6,10},{7,11},{8,12},{9,13},{1... | collective-permute-start | bytes 276488 | tf_op jit(solution)/shard_map/ppermute | solution.py:180
  8.8 3.1 %load.4.refs_2_ = bf16[3584,1024]{1,0:T(8,128)(2,1)S(1)} custom-call(bf16[3584,2048]{1,0:T(8,128)(2,1)} %bitcast.7), custom_call_target="tpu_custom_call" | custom-call | bytes 14680064 | tf_op jit(solution)/shard_map/load/pallas_call | solution.py:79
  11.9 3.1 %load.5.refs_4_ = bf16[3584,1024]{1,0:T(8,128)(2,1)S(1)} custom-call(bf16[3584,2048]{1,0:T(8,128)(2,1)} %bitcast.5), custom_call_target="tpu_custom_call" | custom-call | bytes 14680064 | tf_op jit(solution)/shard_map/load/pallas_call | solution.py:79
  15.0 0.7 %collective-permute-done.1 = bf16[24,1920]{1,0:T(8,128)(2,1)S(1)} collective-permute-done((bf16[24,1920]{1,0:T(8,128)(2,1)S(1)}, bf16[24,1920]{1,0:T(8,128)(2,1)S(1)}, u32[]{:S(2)}, u32[]{:S(2)}) %collective-permute-start.1) | collective-permute-done | bytes 92192 | tf_op jit(solution)/shard_map/ppermute | solution.py:180
  15.7 0.6 %collective-permute-start.4 = (bf16[72,1920]{1,0:T(8,128)(2,1)S(1)}, bf16[72,1920]{1,0:T(8,128)(2,1)S(1)}, u32[]{:S(2)}, u32[]{:S(2)}) collective-permute-start(bf16[72,1920]{1,0:T(8,128)(2,1)S(1)} %pad_maximum_fusion.refs_0_), channel_id=1, source_target_pairs={{0,2},{1,3},{2,0},{3,1},{4,6},{5,7},{6,4},{7,5},{8,10},{9,11},{10,... | collective-permute-start | bytes 829448 | tf_op jit(solution)/shard_map/ppermute | solution.py:180
  16.3 3.1 %load.7.refs_5_ = bf16[3584,1024]{1,0:T(8,128)(2,1)S(1)} custom-call(bf16[3584,2048]{1,0:T(8,128)(2,1)} %bitcast.6, bf16[72,1920]{1,0:T(8,128)(2,1)S(1)} %pad_maximum_fusion.refs_0_), custom_call_target="tpu_custom_call" | custom-call | bytes 14680064 | tf_op jit(solution)/shard_map/load/pallas_call | solution.py:79
  19.4 3.1 %load.6.refs_3_ = bf16[3584,1024]{1,0:T(8,128)(2,1)S(1)} custom-call(bf16[3584,2048]{1,0:T(8,128)(2,1)} %bitcast.8, bf16[72,1920]{1,0:T(8,128)(2,1)S(1)} %pad_maximum_fusion.refs_0_), custom_call_target="tpu_custom_call" | custom-call | bytes 14680064 | tf_op jit(solution)/shard_map/load/pallas_call | solution.py:79
  22.5 1.1 %collective-permute-done.4 = bf16[72,1920]{1,0:T(8,128)(2,1)S(1)} collective-permute-done((bf16[72,1920]{1,0:T(8,128)(2,1)S(1)}, bf16[72,1920]{1,0:T(8,128)(2,1)S(1)}, u32[]{:S(2)}, u32[]{:S(2)}) %collective-permute-start.4) | collective-permute-done | bytes 276512 | tf_op jit(solution)/shard_map/ppermute | solution.py:180
  23.7 2.2 %collective-permute-done.5.refs_1_ = bf16[192,1920]{1,0:T(8,128)(2,1)S(1)} collective-permute-done((bf16[192,1920]{1,0:T(8,128)(2,1)S(1)}, bf16[192,1920]{1,0:T(8,128)(2,1)S(1)}, u32[]{:S(2)}, u32[]{:S(2)}) %collective-permute-start.5) | collective-permute-done | bytes 737312 | tf_op jit(solution)/shard_map/ppermute | solution.py:180
  25.9 8.2 %experts.1 = (bf16[192,896]{1,0:T(8,128)(2,1)S(1)}, bf16[192,896]{1,0:T(8,128)(2,1)S(1)}, bf16[128,2048]{1,0:T(8,128)(2,1)S(1)}, f32[128,128]{1,0:T(8,128)S(1)},...) custom-call(bf16[192,1920]{1,0:T(8,128)(2,1)S(1)} %constant_dynamic-update-slice_fusion.refs_0_, ...), custom_call_target="tpu_custom_call" | custom-call | flops 4697620480 | bytes 29360128 | tf_op jit(solution)/shard_map/experts/pallas_call | solution.py:208
  34.2 0.2 collective-permute-start.6
  34.4 1.5 %project.1 = (bf16[192,896]{1,0:T(8,128)(2,1)S(1)}, bf16[192,896]{1,0:T(8,128)(2,1)S(1)}) custom-call(bf16[128,2048]{1,0:T(8,128)(2,1)S(1)} %get-tuple-element.27.hidden, f32[128,128]{1,0:T(8,128)S(1)} %get-tuple-element.28.weight_ref, bf16[384,256]{1,0:T(8,128)(2,1)S(1)} %get-tuple-element.29.back, bf16[2048,1792]{1,0:T(8,128)(2,1)S(1)} %get-tuple-element.30.down), custom_call_target="tpu_custom_call" | custom-call | flops 939524096 | bytes 7340032 | tf_op jit(solution)/shard_map/project/pallas_call | solution.py:233
  35.8 0.4 collective-permute-start.11
  36.3 0.1 add_convert_fusion.1
  36.4 0.6 %collective-permute-start.7 = (bf16[96,896]{1,0:T(8,128)(2,1)S(1)}, bf16[96,896]{1,0:T(8,128)(2,1)S(1)}, u32[]{:S(2)}, u32[]{:S(2)}) collective-permute-start(bf16[96,896]{1,0:T(8,128)(2,1)S(1)} %slice.67), channel_id=1, source_target_pairs={{0,2},{1,3},{2,0},{3,1},{4,6},{5,7},{6,4},{7,5},{8,10},{9,11},{10,... | collective-permute-start | bytes 516104 | tf_op jit(solution)/shard_map/ppermute | solution.py:180
  36.9 0.6 %collective-permute-done.11 = bf16[192,896]{1,0:T(8,128)(2,1)S(1)} collective-permute-done((bf16[192,896]{1,0:T(8,128)(2,1)S(1)}, bf16[192,896]{1,0:T(8,128)(2,1)S(1)}, u32[]{:S(2)}, u32[]{:S(2)}) %collective-permute-start.11) | collective-permute-done | bytes 344096 | tf_op jit(solution)/shard_map/ppermute | solution.py:180
  37.5 0.1 add_convert_fusion
  37.7 1.0 %collective-permute-start.12 = (bf16[96,896]{1,0:T(8,128)(2,1)S(1)}, bf16[96,896]{1,0:T(8,128)(2,1)S(1)}, u32[]{:S(2)}, u32[]{:S(2)}) collective-permute-start(bf16[96,896]{1,0:T(8,128)(2,1)S(1)} %slice.74), channel_id=1, source_target_pairs={{0,2},{1,3},{2,0},{3,1},{4,6},{5,7},{6,4},{7,5},{8,10},{9,11},{10,... | collective-permute-start | bytes 516104 | tf_op jit(solution)/shard_map/ppermute | solution.py:180
  38.7 5.0 %collective-permute-done.7 = bf16[96,896]{1,0:T(8,128)(2,1)S(1)} collective-permute-done((bf16[96,896]{1,0:T(8,128)(2,1)S(1)}, bf16[96,896]{1,0:T(8,128)(2,1)S(1)}, u32[]{:S(2)}, u32[]{:S(2)}) %collective-permute-start.7) | collective-permute-done | bytes 172064 | tf_op jit(solution)/shard_map/ppermute | solution.py:180
  43.7 1.9 %collective-permute-start.8 = (bf16[24,896]{1,0:T(8,128)(2,1)S(1)}, bf16[24,896]{1,0:T(8,128)(2,1)S(1)}, u32[]{:S(2)}, u32[]{:S(2)}) collective-permute-start(bf16[24,896]{1,0:T(8,128)(2,1)S(1)} %get-tuple-element.33), channel_id=1, source_target_pairs={{0,12},{1,13},{2,14},{3,15},{4,0},{5,1},{6,2},{7,3},{8,4},{9,5},{1... | collective-permute-start | bytes 129032 | tf_op jit(solution)/shard_map/ppermute | solution.py:180
  45.6 0.2 collective-permute-start.10
  45.8 2.2 %collective-permute-start.9 = (bf16[24,896]{1,0:T(8,128)(2,1)S(1)}, bf16[24,896]{1,0:T(8,128)(2,1)S(1)}, u32[]{:S(2)}, u32[]{:S(2)}) collective-permute-start(bf16[24,896]{1,0:T(8,128)(2,1)S(1)} %get-tuple-element.35), channel_id=1, source_target_pairs={{0,8},{1,9},{2,10},{3,11},{4,12},{5,13},{6,14},{7,15},{8,0},{9,1},... | collective-permute-start | bytes 129032 | tf_op jit(solution)/shard_map/ppermute | solution.py:180
  48.1 1.5 %collective-permute-start.13 = (bf16[24,896]{1,0:T(8,128)(2,1)S(1)}, bf16[24,896]{1,0:T(8,128)(2,1)S(1)}, u32[]{:S(2)}, u32[]{:S(2)}) collective-permute-start(bf16[24,896]{1,0:T(8,128)(2,1)S(1)} %get-tuple-element.36), channel_id=1, source_target_pairs={{0,12},{1,13},{2,14},{3,15},{4,0},{5,1},{6,2},{7,3},{8,4},{9,5},{1... | collective-permute-start | bytes 129032 | tf_op jit(solution)/shard_map/ppermute | solution.py:180
  49.5 0.6 %collective-permute-start.15 = (bf16[24,896]{1,0:T(8,128)(2,1)S(1)}, bf16[24,896]{1,0:T(8,128)(2,1)S(1)}, u32[]{:S(2)}, u32[]{:S(2)}) collective-permute-start(bf16[24,896]{1,0:T(8,128)(2,1)S(1)} %get-tuple-element.37), channel_id=1, source_target_pairs={{0,4},{1,5},{2,6},{3,7},{4,8},{5,9},{6,10},{7,11},{8,12},{9,13},{1... | collective-permute-start | bytes 129032 | tf_op jit(solution)/shard_map/ppermute | solution.py:180
  50.2 1.4 %collective-permute-start.14 = (bf16[24,896]{1,0:T(8,128)(2,1)S(1)}, bf16[24,896]{1,0:T(8,128)(2,1)S(1)}, u32[]{:S(2)}, u32[]{:S(2)}) collective-permute-start(bf16[24,896]{1,0:T(8,128)(2,1)S(1)} %get-tuple-element.38), channel_id=1, source_target_pairs={{0,8},{1,9},{2,10},{3,11},{4,12},{5,13},{6,14},{7,15},{8,0},{9,1},... | collective-permute-start | bytes 129032 | tf_op jit(solution)/shard_map/ppermute | solution.py:180
  51.6 1.4 %collective-permute-done.13 = bf16[24,896]{1,0:T(8,128)(2,1)S(1)} collective-permute-done((bf16[24,896]{1,0:T(8,128)(2,1)S(1)}, bf16[24,896]{1,0:T(8,128)(2,1)S(1)}, u32[]{:S(2)}, u32[]{:S(2)}) %collective-permute-start.13) | collective-permute-done | bytes 43040 | tf_op jit(solution)/shard_map/ppermute | solution.py:180
  53.0 2.5 %collective-permute-done.15 = bf16[24,896]{1,0:T(8,128)(2,1)S(1)} collective-permute-done((bf16[24,896]{1,0:T(8,128)(2,1)S(1)}, bf16[24,896]{1,0:T(8,128)(2,1)S(1)}, u32[]{:S(2)}, u32[]{:S(2)}) %collective-permute-start.15) | collective-permute-done | bytes 43040 | tf_op jit(solution)/shard_map/ppermute | solution.py:180
  55.5 0.1 collective-permute-done.14
  55.6 0.7 %pad_maximum_fusion.1 = bf16[12,3584]{1,0:T(8,128)(2,1)} fusion(bf16[12,896]{1,0:T(8,128)(2,1)S(1)} %get-tuple-element.42, bf16[12,896]{1,0:T(8,128)(2,1)S(1)} %get-tuple-element.40, bf16[12,896]{1,0:T(8,128)(2,1)S(1)} %get-tuple-element.41, bf16[12,896]{1,0:T(8,128)(2,1)S(1)} %get-tuple-element.39), kind=kLoop, calls=%fused_computation.5 | loop fusion | flops 344064 | bytes 172032 | tf_op jit(solution)/shard_map/concatenate | solution.py:257
  (27 shorter events, 0.4 us)
Async XLA Ops:
  1.1 21.4 %collective-permute-start.3 = (bf16[24,1920]{1,0:T(8,128)(2,1)S(1)}, bf16[24,1920]{1,0:T(8,128)(2,1)S(1)}, u32[]{:S(2)}, u32[]{:S(2)}) collective-permute-start(bf16[24,1920]{1,0:T(8,128)(2,1)S(1)} %pack.1), channel_id=1, source_target_pairs={{0,2},{1,3},{2,0},{3,1},{4,6},{5,7},{6,4},{7,5},{8,10},{9,11},{10,... | collective-permute-start | bytes 276488 | tf_op jit(solution)/shard_map/ppermute | solution.py:180
  4.2 10.8 %collective-permute-start.2 = (bf16[24,1920]{1,0:T(8,128)(2,1)S(1)}, bf16[24,1920]{1,0:T(8,128)(2,1)S(1)}, u32[]{:S(2)}, u32[]{:S(2)}) collective-permute-start(bf16[24,1920]{1,0:T(8,128)(2,1)S(1)} %pack.1), channel_id=1, source_target_pairs={{0,12},{1,13},{2,14},{3,15},{4,0},{5,1},{6,2},{7,3},{8,4},{9,5},{1... | collective-permute-start | bytes 276488 | tf_op jit(solution)/shard_map/ppermute | solution.py:180
  7.8 7.9 %collective-permute-start.1 = (bf16[24,1920]{1,0:T(8,128)(2,1)S(1)}, bf16[24,1920]{1,0:T(8,128)(2,1)S(1)}, u32[]{:S(2)}, u32[]{:S(2)}) collective-permute-start(bf16[24,1920]{1,0:T(8,128)(2,1)S(1)} %pack.1), channel_id=1, source_target_pairs={{0,8},{1,9},{2,10},{3,11},{4,12},{5,13},{6,14},{7,15},{8,0},{9,1},... | collective-permute-start | bytes 276488 | tf_op jit(solution)/shard_map/ppermute | solution.py:180
  7.8 7.9 %collective-permute-start = (bf16[24,1920]{1,0:T(8,128)(2,1)S(1)}, bf16[24,1920]{1,0:T(8,128)(2,1)S(1)}, u32[]{:S(2)}, u32[]{:S(2)}) collective-permute-start(bf16[24,1920]{1,0:T(8,128)(2,1)S(1)} %pack.1), channel_id=1, source_target_pairs={{0,4},{1,5},{2,6},{3,7},{4,8},{5,9},{6,10},{7,11},{8,12},{9,13},{1... | collective-permute-start | bytes 276488 | tf_op jit(solution)/shard_map/ppermute | solution.py:180
  15.7 7.9 %collective-permute-start.4 = (bf16[72,1920]{1,0:T(8,128)(2,1)S(1)}, bf16[72,1920]{1,0:T(8,128)(2,1)S(1)}, u32[]{:S(2)}, u32[]{:S(2)}) collective-permute-start(bf16[72,1920]{1,0:T(8,128)(2,1)S(1)} %pad_maximum_fusion.refs_0_), channel_id=1, source_target_pairs={{0,2},{1,3},{2,0},{3,1},{4,6},{5,7},{6,4},{7,5},{8,10},{9,11},{10,... | collective-permute-start | bytes 829448 | tf_op jit(solution)/shard_map/ppermute | solution.py:180
  23.7 2.3 %collective-permute-start.5 = (bf16[192,1920]{1,0:T(8,128)(2,1)S(1)}, bf16[192,1920]{1,0:T(8,128)(2,1)S(1)}, u32[]{:S(2)}, u32[]{:S(2)}) collective-permute-start(bf16[192,1920]{1,0:T(8,128)(2,1)S(1)} %constant_dynamic-update-slice_fusion.refs_0_), channel_id=1, source_target_pairs={{0,1},{1,0},{2,3},{3,2},{4,5},{5,4},{6,7},{7,6},{8,9},{9,8},{10,11... | collective-permute-start | bytes 2211848 | tf_op jit(solution)/shard_map/ppermute | solution.py:180
  34.2 2.1 %collective-permute-start.6 = (bf16[192,896]{1,0:T(8,128)(2,1)S(1)}, bf16[192,896]{1,0:T(8,128)(2,1)S(1)}, u32[]{:S(2)}, u32[]{:S(2)}) collective-permute-start(bf16[192,896]{1,0:T(8,128)(2,1)S(1)} %get-tuple-element.26), channel_id=1, source_target_pairs={{0,1},{1,0},{2,3},{3,2},{4,5},{5,4},{6,7},{7,6},{8,9},{9,8},{10,11... | collective-permute-start | bytes 1032200 | tf_op jit(solution)/shard_map/ppermute | solution.py:180
  35.8 1.7 %collective-permute-start.11 = (bf16[192,896]{1,0:T(8,128)(2,1)S(1)}, bf16[192,896]{1,0:T(8,128)(2,1)S(1)}, u32[]{:S(2)}, u32[]{:S(2)}) collective-permute-start(bf16[192,896]{1,0:T(8,128)(2,1)S(1)} %get-tuple-element.32), channel_id=1, source_target_pairs={{0,1},{1,0},{2,3},{3,2},{4,5},{5,4},{6,7},{7,6},{8,9},{9,8},{10,11... | collective-permute-start | bytes 1032200 | tf_op jit(solution)/shard_map/ppermute | solution.py:180
  36.4 7.3 %collective-permute-start.7 = (bf16[96,896]{1,0:T(8,128)(2,1)S(1)}, bf16[96,896]{1,0:T(8,128)(2,1)S(1)}, u32[]{:S(2)}, u32[]{:S(2)}) collective-permute-start(bf16[96,896]{1,0:T(8,128)(2,1)S(1)} %slice.67), channel_id=1, source_target_pairs={{0,2},{1,3},{2,0},{3,1},{4,6},{5,7},{6,4},{7,5},{8,10},{9,11},{10,... | collective-permute-start | bytes 516104 | tf_op jit(solution)/shard_map/ppermute | solution.py:180
  37.7 10.3 %collective-permute-start.12 = (bf16[96,896]{1,0:T(8,128)(2,1)S(1)}, bf16[96,896]{1,0:T(8,128)(2,1)S(1)}, u32[]{:S(2)}, u32[]{:S(2)}) collective-permute-start(bf16[96,896]{1,0:T(8,128)(2,1)S(1)} %slice.74), channel_id=1, source_target_pairs={{0,2},{1,3},{2,0},{3,1},{4,6},{5,7},{6,4},{7,5},{8,10},{9,11},{10,... | collective-permute-start | bytes 516104 | tf_op jit(solution)/shard_map/ppermute | solution.py:180
  43.7 6.4 %collective-permute-start.8 = (bf16[24,896]{1,0:T(8,128)(2,1)S(1)}, bf16[24,896]{1,0:T(8,128)(2,1)S(1)}, u32[]{:S(2)}, u32[]{:S(2)}) collective-permute-start(bf16[24,896]{1,0:T(8,128)(2,1)S(1)} %get-tuple-element.33), channel_id=1, source_target_pairs={{0,12},{1,13},{2,14},{3,15},{4,0},{5,1},{6,2},{7,3},{8,4},{9,5},{1... | collective-permute-start | bytes 129032 | tf_op jit(solution)/shard_map/ppermute | solution.py:180
  45.6 6.0 %collective-permute-start.10 = (bf16[24,896]{1,0:T(8,128)(2,1)S(1)}, bf16[24,896]{1,0:T(8,128)(2,1)S(1)}, u32[]{:S(2)}, u32[]{:S(2)}) collective-permute-start(bf16[24,896]{1,0:T(8,128)(2,1)S(1)} %get-tuple-element.34), channel_id=1, source_target_pairs={{0,4},{1,5},{2,6},{3,7},{4,8},{5,9},{6,10},{7,11},{8,12},{9,13},{1... | collective-permute-start | bytes 129032 | tf_op jit(solution)/shard_map/ppermute | solution.py:180
  45.8 5.8 %collective-permute-start.9 = (bf16[24,896]{1,0:T(8,128)(2,1)S(1)}, bf16[24,896]{1,0:T(8,128)(2,1)S(1)}, u32[]{:S(2)}, u32[]{:S(2)}) collective-permute-start(bf16[24,896]{1,0:T(8,128)(2,1)S(1)} %get-tuple-element.35), channel_id=1, source_target_pairs={{0,8},{1,9},{2,10},{3,11},{4,12},{5,13},{6,14},{7,15},{8,0},{9,1},... | collective-permute-start | bytes 129032 | tf_op jit(solution)/shard_map/ppermute | solution.py:180
  48.1 4.9 %collective-permute-start.13 = (bf16[24,896]{1,0:T(8,128)(2,1)S(1)}, bf16[24,896]{1,0:T(8,128)(2,1)S(1)}, u32[]{:S(2)}, u32[]{:S(2)}) collective-permute-start(bf16[24,896]{1,0:T(8,128)(2,1)S(1)} %get-tuple-element.36), channel_id=1, source_target_pairs={{0,12},{1,13},{2,14},{3,15},{4,0},{5,1},{6,2},{7,3},{8,4},{9,5},{1... | collective-permute-start | bytes 129032 | tf_op jit(solution)/shard_map/ppermute | solution.py:180
  49.5 5.9 %collective-permute-start.15 = (bf16[24,896]{1,0:T(8,128)(2,1)S(1)}, bf16[24,896]{1,0:T(8,128)(2,1)S(1)}, u32[]{:S(2)}, u32[]{:S(2)}) collective-permute-start(bf16[24,896]{1,0:T(8,128)(2,1)S(1)} %get-tuple-element.37), channel_id=1, source_target_pairs={{0,4},{1,5},{2,6},{3,7},{4,8},{5,9},{6,10},{7,11},{8,12},{9,13},{1... | collective-permute-start | bytes 129032 | tf_op jit(solution)/shard_map/ppermute | solution.py:180
  50.2 5.4 %collective-permute-start.14 = (bf16[24,896]{1,0:T(8,128)(2,1)S(1)}, bf16[24,896]{1,0:T(8,128)(2,1)S(1)}, u32[]{:S(2)}, u32[]{:S(2)}) collective-permute-start(bf16[24,896]{1,0:T(8,128)(2,1)S(1)} %get-tuple-element.38), channel_id=1, source_target_pairs={{0,8},{1,9},{2,10},{3,11},{4,12},{5,13},{6,14},{7,15},{8,0},{9,1},... | collective-permute-start | bytes 129032 | tf_op jit(solution)/shard_map/ppermute | solution.py:180
where the time goes:
time: 56.5 us; the launch traced here: 56.3 us
  Pallas kernels  23.2 us (41%)
  starting transfers between devices  18.3 us (32%)
  waiting for transfers between devices  13.5 us (24%)
  other arithmetic  0.99 us (2%)
    ppermute x16, starting transfers between devices, send(): return lax.ppermute(x, 'expert', pairs)  18.3 us
    ppermute x16, waiting for transfers between devices, send(): return lax.ppermute(x, 'expert', pairs)  13.5 us
    pallas_call x4, Pallas kernels, load(): pl.pallas_call(functools.partial(load_kernel, spans), out_shape=pltpu.VME...  12.4 us
    pallas_call x1, Pallas kernels, body(): pl.pallas_call(functools.partial(expert_kernel, rows, 2, len(gates), span...  8.21 us
    pallas_call x1, Pallas kernels, body(): pl.pallas_call(project_kernel, out_shape=outs, in_specs=[IN_VMEM] * 4, ou...  1.46 us
  transfers between devices with their start and end apart: 16, of which 8 were waited for; matrix products, arithmetic and copies ran while one was open for 1% of the time, Pallas kernels for 25%

commit v1 on v0

--- a/solution.py
+++ b/solution.py
@@ -190,19 +190,21 @@
         out_shape=pltpu.VMEM((block, half + LANES), BF16),
         name="pack",
     )(tokens, expert_ids.T, gate_weights.T)
-    low, high = [(0, units // 2)], [(units // 2, units // 2)]
-    gates, ups = [load(w_gate[0], low)], [load(w_up[0], low)]
+    gates = [load(w_gate[0], [(0, units)])]
     spans = [(c * span + h * half, span) for c in range(CHUNKS) for h in range(2)]
 
     shifted = [send(own, shift(s)) for s in range(1, steps)]
     across = send(own, flip_second)
     column = jnp.concatenate([own] + shifted, axis=0)
-    onward, gates[0], ups[0] = lax.optimization_barrier((column[block:], gates[0], ups[0]))
-    plane = jnp.concatenate([column, across, send(onward, flip_second)], axis=0)
-    gates.append(load(w_gate[0], high, onward))
-    ups.append(load(w_up[0], high, onward))
-    plane, gates[1], ups[1] = lax.optimization_barrier((plane, gates[1], ups[1]))
-    other = send(plane, flip_core)
+    column, across, gates[0] = lax.optimization_barrier((column, across, gates[0]))
+    onward = column[block:]
+    rest = send(onward, flip_second)
+    column_of_core = send(column, flip_core)
+    ups = [load(w_up[0], [(0, units)], onward)]
+    second = jnp.concatenate([across, rest], axis=0)
+    second, column_of_core, ups[0] = lax.optimization_barrier((second, column_of_core, ups[0]))
+    plane = jnp.concatenate([column, second], axis=0)
+    other = jnp.concatenate([column_of_core, send(second, flip_core)], axis=0)
 
     outs = [pltpu.VMEM((count // 2, span), BF16)] * 2
     keep, away, hidden, weight, back, *downs = pl.pallas_call(
@@ -221,7 +223,7 @@
             pltpu.VMEM((units, 2 * span), BF16),
             pltpu.SemaphoreType.DMA((len(spans),)),
         ],
-        compiler_params=pltpu.CompilerParams(vmem_limit_bytes=14 * MIB),
+        compiler_params=pltpu.CompilerParams(vmem_limit_bytes=10 * MIB),
         cost_estimate=pl.CostEstimate(
             flops=5 * slots * width * units, bytes_accessed=4 * width * units, transcendentals=slots * units
         ),
@@ -235,7 +237,7 @@
                 out_shape=outs,
                 in_specs=[IN_VMEM] * 4,
                 out_specs=[IN_VMEM] * 2,
-                compiler_params=pltpu.CompilerParams(vmem_limit_bytes=14 * MIB),
+                compiler_params=pltpu.CompilerParams(vmem_limit_bytes=10 * MIB),
                 cost_estimate=pl.CostEstimate(
                     flops=slots * width * units, bytes_accessed=width * units, transcendentals=0
                 ),

time: 56.5 us -> 54.1 us (0.958)
  Pallas kernels: 23.2 us -> 20.2 us
  starting transfers between devices: 18.3 us -> 20.4 us
  waiting for transfers between devices: 13.5 us -> 11.9 us
    ppermute x16 -> x17, starting transfers between devices: 18.3 us -> 20.4 us  [send(): return lax.ppermute(x, 'expert', pairs)]
    pallas_call x4 -> x2, Pallas kernels: 12.4 us -> 10.4 us  [load(): pl.pallas_call(functools.partial(load_kernel, spans), out_shape=pltpu.VME...]
    ppermute x16 -> x17, waiting for transfers between devices: 13.5 us -> 11.9 us  [send(): return lax.ppermute(x, 'expert', pairs)]
    pallas_call x1, Pallas kernels: 8.21 us -> 7.28 us  [body(): pl.pallas_call(functools.partial(expert_kernel, rows, 2, len(gates), span...]
  transfers between devices with their start and end apart: 16 -> 17, of which waited for: 8 -> 7; matrix products, arithmetic and copies ran while one was open for 1% -> 1% of each run, Pallas kernels for 25% -> 22%
where the time goes in v1:
time: 54.1 us; the launch traced here: 53.9 us
  starting transfers between devices  20.4 us (38%)
  Pallas kernels  20.2 us (37%)
  waiting for transfers between devices  11.9 us (22%)
  other arithmetic  1.15 us (2%)
    ppermute x17, starting transfers between devices, send(): return lax.ppermute(x, 'expert', pairs)  20.4 us
    ppermute x17, waiting for transfers between devices, send(): return lax.ppermute(x, 'expert', pairs)  11.9 us
    pallas_call x2, Pallas kernels, load(): pl.pallas_call(functools.partial(load_kernel, spans), out_shape=pltpu.VME...  10.4 us
    pallas_call x1, Pallas kernels, body(): pl.pallas_call(functools.partial(expert_kernel, rows, 2, len(gates), span...  7.28 us
    pallas_call x1, Pallas kernels, body(): pl.pallas_call(project_kernel, out_shape=outs, in_specs=[IN_VMEM] * 4, ou...  1.46 us
    pallas_call x1, Pallas kernels, body(): pl.pallas_call(pack_kernel, out_shape=pltpu.VMEM((block, half + LANES), B...  1.12 us
  transfers between devices with their start and end apart: 17, of which 7 were waited for; matrix products, arithmetic and copies ran while one was open for 1% of the time, Pallas kernels for 22%

profile of v1, /device:TPU:0, one launch (start us, length us, event | category | flops | bytes accessed | tf_op | source)
XLA Modules:
  0.0 53.9 jit_solution(5993424889483458100)
XLA Ops:
  0.0 1.1 %pack.1 = bf16[24,1920]{1,0:T(8,128)(2,1)S(1)} custom-call(bf16[12,3584]{1,0:T(8,128)(2,1)} %tokens_ref.1, s32[8,12]{1,0:T(8,128)} %bitcast.8, f32[8,12]{1,0:T(8,128)} %bitcast.9), custom_call_target="tpu_custom_call" | custom-call | tf_op jit(solution)/shard_map/pack/pallas_call | solution.py:188
  1.1 5.1 %collective-permute-start.2 = (bf16[24,1920]{1,0:T(8,128)(2,1)S(1)}, bf16[24,1920]{1,0:T(8,128)(2,1)S(1)}, u32[]{:S(2)}, u32[]{:S(2)}) collective-permute-start(bf16[24,1920]{1,0:T(8,128)(2,1)S(1)} %pack.1), channel_id=1, source_target_pairs={{0,12},{1,13},{2,14},{3,15},{4,0},{5,1},{6,2},{7,3},{8,4},{9,5},{1... | collective-permute-start | bytes 276488 | tf_op jit(solution)/shard_map/ppermute | solution.py:180
  6.2 1.0 %collective-permute-start = (bf16[24,1920]{1,0:T(8,128)(2,1)S(1)}, bf16[24,1920]{1,0:T(8,128)(2,1)S(1)}, u32[]{:S(2)}, u32[]{:S(2)}) collective-permute-start(bf16[24,1920]{1,0:T(8,128)(2,1)S(1)} %pack.1), channel_id=1, source_target_pairs={{0,4},{1,5},{2,6},{3,7},{4,8},{5,9},{6,10},{7,11},{8,12},{9,13},{1... | collective-permute-start | bytes 276488 | tf_op jit(solution)/shard_map/ppermute | solution.py:180
  7.2 1.5 %collective-permute-start.3 = (bf16[24,1920]{1,0:T(8,128)(2,1)S(1)}, bf16[24,1920]{1,0:T(8,128)(2,1)S(1)}, u32[]{:S(2)}, u32[]{:S(2)}) collective-permute-start(bf16[24,1920]{1,0:T(8,128)(2,1)S(1)} %pack.1), channel_id=1, source_target_pairs={{0,2},{1,3},{2,0},{3,1},{4,6},{5,7},{6,4},{7,5},{8,10},{9,11},{10,... | collective-permute-start | bytes 276488 | tf_op jit(solution)/shard_map/ppermute | solution.py:180
  8.8 5.2 %load.2.refs_2_ = bf16[3584,2048]{1,0:T(8,128)(2,1)S(1)} custom-call(bf16[3584,2048]{1,0:T(8,128)(2,1)} %bitcast.5), custom_call_target="tpu_custom_call" | custom-call | bytes 29360128 | tf_op jit(solution)/shard_map/load/pallas_call | solution.py:79
  14.0 0.6 %collective-permute-done.1 = bf16[24,1920]{1,0:T(8,128)(2,1)S(1)} collective-permute-done((bf16[24,1920]{1,0:T(8,128)(2,1)S(1)}, bf16[24,1920]{1,0:T(8,128)(2,1)S(1)}, u32[]{:S(2)}, u32[]{:S(2)}) %collective-permute-start.1) | collective-permute-done | bytes 92192 | tf_op jit(solution)/shard_map/ppermute | solution.py:180
  14.6 1.6 %collective-permute-start.4 = (bf16[72,1920]{1,0:T(8,128)(2,1)S(1)}, bf16[72,1920]{1,0:T(8,128)(2,1)S(1)}, u32[]{:S(2)}, u32[]{:S(2)}) collective-permute-start(bf16[72,1920]{1,0:T(8,128)(2,1)S(1)} %slice.51.refs_0_), channel_id=1, source_target_pairs={{0,2},{1,3},{2,0},{3,1},{4,6},{5,7},{6,4},{7,5},{8,10},{9,11},{10,... | collective-permute-start | bytes 829448 | tf_op jit(solution)/shard_map/ppermute | solution.py:180
  16.2 5.2 %load.3.refs_3_ = bf16[3584,2048]{1,0:T(8,128)(2,1)S(1)} custom-call(bf16[3584,2048]{1,0:T(8,128)(2,1)} %bitcast.6, bf16[72,1920]{1,0:T(8,128)(2,1)S(1)} %slice.51.refs_0_), custom_call_target="tpu_custom_call" | custom-call | bytes 29360128 | tf_op jit(solution)/shard_map/load/pallas_call | solution.py:79
  21.4 1.4 %collective-permute-done.4 = bf16[72,1920]{1,0:T(8,128)(2,1)S(1)} collective-permute-done((bf16[72,1920]{1,0:T(8,128)(2,1)S(1)}, bf16[72,1920]{1,0:T(8,128)(2,1)S(1)}, u32[]{:S(2)}, u32[]{:S(2)}) %collective-permute-start.4) | collective-permute-done | bytes 276512 | tf_op jit(solution)/shard_map/ppermute | solution.py:180
  22.8 0.1 collective-permute-start.6
  22.9 0.1 pad_maximum_fusion.refs_0_
  23.0 1.6 %collective-permute-done.6 = bf16[96,1920]{1,0:T(8,128)(2,1)S(1)} collective-permute-done((bf16[96,1920]{1,0:T(8,128)(2,1)S(1)}, bf16[96,1920]{1,0:T(8,128)(2,1)S(1)}, u32[]{:S(2)}, u32[]{:S(2)}) %collective-permute-start.6) | collective-permute-done | bytes 368672 | tf_op jit(solution)/shard_map/ppermute | solution.py:180
  24.6 0.1 pad_maximum_fusion.1.refs_1_
  24.6 7.3 %experts.1 = (bf16[192,896]{1,0:T(8,128)(2,1)S(1)}, bf16[192,896]{1,0:T(8,128)(2,1)S(1)}, bf16[128,2048]{1,0:T(8,128)(2,1)S(1)}, f32[128,128]{1,0:T(8,128)S(1)},...) custom-call(bf16[192,1920]{1,0:T(8,128)(2,1)S(1)} %pad_maximum_fusion.refs_0_, ...), custom_call_target="tpu_custom_call" | custom-call | flops 4697620480 | bytes 29360128 | tf_op jit(solution)/shard_map/experts/pallas_call | solution.py:210
  31.9 0.2 collective-permute-start.7
  32.1 1.5 %project.1 = (bf16[192,896]{1,0:T(8,128)(2,1)S(1)}, bf16[192,896]{1,0:T(8,128)(2,1)S(1)}) custom-call(bf16[128,2048]{1,0:T(8,128)(2,1)S(1)} %get-tuple-element.27.hidden, f32[128,128]{1,0:T(8,128)S(1)} %get-tuple-element.28.weight_ref, bf16[384,256]{1,0:T(8,128)(2,1)S(1)} %get-tuple-element.29.back, bf16[2048,1792]{1,0:T(8,128)(2,1)S(1)} %get-tuple-element.30.down), custom_call_target="tpu_custom_call" | custom-call | flops 939524096 | bytes 7340032 | tf_op jit(solution)/shard_map/project/pallas_call | solution.py:235
  33.6 0.4 collective-permute-start.12
  34.0 0.1 add_convert_fusion.1
  34.1 1.6 %collective-permute-start.8 = (bf16[96,896]{1,0:T(8,128)(2,1)S(1)}, bf16[96,896]{1,0:T(8,128)(2,1)S(1)}, u32[]{:S(2)}, u32[]{:S(2)}) collective-permute-start(bf16[96,896]{1,0:T(8,128)(2,1)S(1)} %slice.69), channel_id=1, source_target_pairs={{0,2},{1,3},{2,0},{3,1},{4,6},{5,7},{6,4},{7,5},{8,10},{9,11},{10,... | collective-permute-start | bytes 516104 | tf_op jit(solution)/shard_map/ppermute | solution.py:180
  35.7 0.1 add_convert_fusion
  35.9 1.2 %collective-permute-start.13 = (bf16[96,896]{1,0:T(8,128)(2,1)S(1)}, bf16[96,896]{1,0:T(8,128)(2,1)S(1)}, u32[]{:S(2)}, u32[]{:S(2)}) collective-permute-start(bf16[96,896]{1,0:T(8,128)(2,1)S(1)} %slice.76), channel_id=1, source_target_pairs={{0,2},{1,3},{2,0},{3,1},{4,6},{5,7},{6,4},{7,5},{8,10},{9,11},{10,... | collective-permute-start | bytes 516104 | tf_op jit(solution)/shard_map/ppermute | solution.py:180
  37.0 4.4 %collective-permute-done.8 = bf16[96,896]{1,0:T(8,128)(2,1)S(1)} collective-permute-done((bf16[96,896]{1,0:T(8,128)(2,1)S(1)}, bf16[96,896]{1,0:T(8,128)(2,1)S(1)}, u32[]{:S(2)}, u32[]{:S(2)}) %collective-permute-start.8) | collective-permute-done | bytes 172064 | tf_op jit(solution)/shard_map/ppermute | solution.py:180
  41.5 1.7 %collective-permute-start.9 = (bf16[24,896]{1,0:T(8,128)(2,1)S(1)}, bf16[24,896]{1,0:T(8,128)(2,1)S(1)}, u32[]{:S(2)}, u32[]{:S(2)}) collective-permute-start(bf16[24,896]{1,0:T(8,128)(2,1)S(1)} %get-tuple-element.33), channel_id=1, source_target_pairs={{0,12},{1,13},{2,14},{3,15},{4,0},{5,1},{6,2},{7,3},{8,4},{9,5},{1... | collective-permute-start | bytes 129032 | tf_op jit(solution)/shard_map/ppermute | solution.py:180
  43.2 0.3 collective-permute-start.11
  43.6 1.9 %collective-permute-start.10 = (bf16[24,896]{1,0:T(8,128)(2,1)S(1)}, bf16[24,896]{1,0:T(8,128)(2,1)S(1)}, u32[]{:S(2)}, u32[]{:S(2)}) collective-permute-start(bf16[24,896]{1,0:T(8,128)(2,1)S(1)} %get-tuple-element.35), channel_id=1, source_target_pairs={{0,8},{1,9},{2,10},{3,11},{4,12},{5,13},{6,14},{7,15},{8,0},{9,1},... | collective-permute-start | bytes 129032 | tf_op jit(solution)/shard_map/ppermute | solution.py:180
  45.5 1.7 %collective-permute-start.14 = (bf16[24,896]{1,0:T(8,128)(2,1)S(1)}, bf16[24,896]{1,0:T(8,128)(2,1)S(1)}, u32[]{:S(2)}, u32[]{:S(2)}) collective-permute-start(bf16[24,896]{1,0:T(8,128)(2,1)S(1)} %get-tuple-element.36), channel_id=1, source_target_pairs={{0,12},{1,13},{2,14},{3,15},{4,0},{5,1},{6,2},{7,3},{8,4},{9,5},{1... | collective-permute-start | bytes 129032 | tf_op jit(solution)/shard_map/ppermute | solution.py:180
  47.2 0.6 %collective-permute-start.16 = (bf16[24,896]{1,0:T(8,128)(2,1)S(1)}, bf16[24,896]{1,0:T(8,128)(2,1)S(1)}, u32[]{:S(2)}, u32[]{:S(2)}) collective-permute-start(bf16[24,896]{1,0:T(8,128)(2,1)S(1)} %get-tuple-element.37), channel_id=1, source_target_pairs={{0,4},{1,5},{2,6},{3,7},{4,8},{5,9},{6,10},{7,11},{8,12},{9,13},{1... | collective-permute-start | bytes 129032 | tf_op jit(solution)/shard_map/ppermute | solution.py:180
  47.8 1.4 %collective-permute-start.15 = (bf16[24,896]{1,0:T(8,128)(2,1)S(1)}, bf16[24,896]{1,0:T(8,128)(2,1)S(1)}, u32[]{:S(2)}, u32[]{:S(2)}) collective-permute-start(bf16[24,896]{1,0:T(8,128)(2,1)S(1)} %get-tuple-element.38), channel_id=1, source_target_pairs={{0,8},{1,9},{2,10},{3,11},{4,12},{5,13},{6,14},{7,15},{8,0},{9,1},... | collective-permute-start | bytes 129032 | tf_op jit(solution)/shard_map/ppermute | solution.py:180
  49.3 1.3 %collective-permute-done.14 = bf16[24,896]{1,0:T(8,128)(2,1)S(1)} collective-permute-done((bf16[24,896]{1,0:T(8,128)(2,1)S(1)}, bf16[24,896]{1,0:T(8,128)(2,1)S(1)}, u32[]{:S(2)}, u32[]{:S(2)}) %collective-permute-start.14) | collective-permute-done | bytes 43040 | tf_op jit(solution)/shard_map/ppermute | solution.py:180
  50.6 2.5 %collective-permute-done.16 = bf16[24,896]{1,0:T(8,128)(2,1)S(1)} collective-permute-done((bf16[24,896]{1,0:T(8,128)(2,1)S(1)}, bf16[24,896]{1,0:T(8,128)(2,1)S(1)}, u32[]{:S(2)}, u32[]{:S(2)}) %collective-permute-start.16) | collective-permute-done | bytes 43040 | tf_op jit(solution)/shard_map/ppermute | solution.py:180
  53.1 0.1 collective-permute-done.15
  53.3 0.7 %pad_maximum_fusion.4 = bf16[12,3584]{1,0:T(8,128)(2,1)} fusion(bf16[12,896]{1,0:T(8,128)(2,1)S(1)} %get-tuple-element.42, bf16[12,896]{1,0:T(8,128)(2,1)S(1)} %get-tuple-element.40, bf16[12,896]{1,0:T(8,128)(2,1)S(1)} %get-tuple-element.41, bf16[12,896]{1,0:T(8,128)(2,1)S(1)} %get-tuple-element.39), kind=kLoop, calls=%fused_computation.8 | loop fusion | flops 344064 | bytes 172032 | tf_op jit(solution)/shard_map/concatenate | solution.py:259
  (25 shorter events, 0.3 us)
Async XLA Ops:
  1.1 12.8 %collective-permute-start.2 = (bf16[24,1920]{1,0:T(8,128)(2,1)S(1)}, bf16[24,1920]{1,0:T(8,128)(2,1)S(1)}, u32[]{:S(2)}, u32[]{:S(2)}) collective-permute-start(bf16[24,1920]{1,0:T(8,128)(2,1)S(1)} %pack.1), channel_id=1, source_target_pairs={{0,12},{1,13},{2,14},{3,15},{4,0},{5,1},{6,2},{7,3},{8,4},{9,5},{1... | collective-permute-start | bytes 276488 | tf_op jit(solution)/shard_map/ppermute | solution.py:180
  6.2 8.3 %collective-permute-start.1 = (bf16[24,1920]{1,0:T(8,128)(2,1)S(1)}, bf16[24,1920]{1,0:T(8,128)(2,1)S(1)}, u32[]{:S(2)}, u32[]{:S(2)}) collective-permute-start(bf16[24,1920]{1,0:T(8,128)(2,1)S(1)} %pack.1), channel_id=1, source_target_pairs={{0,8},{1,9},{2,10},{3,11},{4,12},{5,13},{6,14},{7,15},{8,0},{9,1},... | collective-permute-start | bytes 276488 | tf_op jit(solution)/shard_map/ppermute | solution.py:180
  6.2 8.3 %collective-permute-start = (bf16[24,1920]{1,0:T(8,128)(2,1)S(1)}, bf16[24,1920]{1,0:T(8,128)(2,1)S(1)}, u32[]{:S(2)}, u32[]{:S(2)}) collective-permute-start(bf16[24,1920]{1,0:T(8,128)(2,1)S(1)} %pack.1), channel_id=1, source_target_pairs={{0,4},{1,5},{2,6},{3,7},{4,8},{5,9},{6,10},{7,11},{8,12},{9,13},{1... | collective-permute-start | bytes 276488 | tf_op jit(solution)/shard_map/ppermute | solution.py:180
  7.2 7.3 %collective-permute-start.3 = (bf16[24,1920]{1,0:T(8,128)(2,1)S(1)}, bf16[24,1920]{1,0:T(8,128)(2,1)S(1)}, u32[]{:S(2)}, u32[]{:S(2)}) collective-permute-start(bf16[24,1920]{1,0:T(8,128)(2,1)S(1)} %pack.1), channel_id=1, source_target_pairs={{0,2},{1,3},{2,0},{3,1},{4,6},{5,7},{6,4},{7,5},{8,10},{9,11},{10,... | collective-permute-start | bytes 276488 | tf_op jit(solution)/shard_map/ppermute | solution.py:180
  14.6 8.2 %collective-permute-start.4 = (bf16[72,1920]{1,0:T(8,128)(2,1)S(1)}, bf16[72,1920]{1,0:T(8,128)(2,1)S(1)}, u32[]{:S(2)}, u32[]{:S(2)}) collective-permute-start(bf16[72,1920]{1,0:T(8,128)(2,1)S(1)} %slice.51.refs_0_), channel_id=1, source_target_pairs={{0,2},{1,3},{2,0},{3,1},{4,6},{5,7},{6,4},{7,5},{8,10},{9,11},{10,... | collective-permute-start | bytes 829448 | tf_op jit(solution)/shard_map/ppermute | solution.py:180
  16.2 6.6 %collective-permute-start.5 = (bf16[96,1920]{1,0:T(8,128)(2,1)S(1)}, bf16[96,1920]{1,0:T(8,128)(2,1)S(1)}, u32[]{:S(2)}, u32[]{:S(2)}) collective-permute-start(bf16[96,1920]{1,0:T(8,128)(2,1)S(1)} %pad_maximum_fusion.2), channel_id=1, source_target_pairs={{0,1},{1,0},{2,3},{3,2},{4,5},{5,4},{6,7},{7,6},{8,9},{9,8},{10,11... | collective-permute-start | bytes 1105928 | tf_op jit(solution)/shard_map/ppermute | solution.py:180
  22.8 1.8 %collective-permute-start.6 = (bf16[96,1920]{1,0:T(8,128)(2,1)S(1)}, bf16[96,1920]{1,0:T(8,128)(2,1)S(1)}, u32[]{:S(2)}, u32[]{:S(2)}) collective-permute-start(bf16[96,1920]{1,0:T(8,128)(2,1)S(1)} %pad_maximum_fusion.3), channel_id=1, source_target_pairs={{0,1},{1,0},{2,3},{3,2},{4,5},{5,4},{6,7},{7,6},{8,9},{9,8},{10,11... | collective-permute-start | bytes 1105928 | tf_op jit(solution)/shard_map/ppermute | solution.py:180
  31.9 2.1 %collective-permute-start.7 = (bf16[192,896]{1,0:T(8,128)(2,1)S(1)}, bf16[192,896]{1,0:T(8,128)(2,1)S(1)}, u32[]{:S(2)}, u32[]{:S(2)}) collective-permute-start(bf16[192,896]{1,0:T(8,128)(2,1)S(1)} %get-tuple-element.26), channel_id=1, source_target_pairs={{0,1},{1,0},{2,3},{3,2},{4,5},{5,4},{6,7},{7,6},{8,9},{9,8},{10,11... | collective-permute-start | bytes 1032200 | tf_op jit(solution)/shard_map/ppermute | solution.py:180
  33.6 2.1 %collective-permute-start.12 = (bf16[192,896]{1,0:T(8,128)(2,1)S(1)}, bf16[192,896]{1,0:T(8,128)(2,1)S(1)}, u32[]{:S(2)}, u32[]{:S(2)}) collective-permute-start(bf16[192,896]{1,0:T(8,128)(2,1)S(1)} %get-tuple-element.32), channel_id=1, source_target_pairs={{0,1},{1,0},{2,3},{3,2},{4,5},{5,4},{6,7},{7,6},{8,9},{9,8},{10,11... | collective-permute-start | bytes 1032200 | tf_op jit(solution)/shard_map/ppermute | solution.py:180
  34.1 7.3 %collective-permute-start.8 = (bf16[96,896]{1,0:T(8,128)(2,1)S(1)}, bf16[96,896]{1,0:T(8,128)(2,1)S(1)}, u32[]{:S(2)}, u32[]{:S(2)}) collective-permute-start(bf16[96,896]{1,0:T(8,128)(2,1)S(1)} %slice.69), channel_id=1, source_target_pairs={{0,2},{1,3},{2,0},{3,1},{4,6},{5,7},{6,4},{7,5},{8,10},{9,11},{10,... | collective-permute-start | bytes 516104 | tf_op jit(solution)/shard_map/ppermute | solution.py:180
  35.9 9.6 %collective-permute-start.13 = (bf16[96,896]{1,0:T(8,128)(2,1)S(1)}, bf16[96,896]{1,0:T(8,128)(2,1)S(1)}, u32[]{:S(2)}, u32[]{:S(2)}) collective-permute-start(bf16[96,896]{1,0:T(8,128)(2,1)S(1)} %slice.76), channel_id=1, source_target_pairs={{0,2},{1,3},{2,0},{3,1},{4,6},{5,7},{6,4},{7,5},{8,10},{9,11},{10,... | collective-permute-start | bytes 516104 | tf_op jit(solution)/shard_map/ppermute | solution.py:180
  41.5 6.3 %collective-permute-start.9 = (bf16[24,896]{1,0:T(8,128)(2,1)S(1)}, bf16[24,896]{1,0:T(8,128)(2,1)S(1)}, u32[]{:S(2)}, u32[]{:S(2)}) collective-permute-start(bf16[24,896]{1,0:T(8,128)(2,1)S(1)} %get-tuple-element.33), channel_id=1, source_target_pairs={{0,12},{1,13},{2,14},{3,15},{4,0},{5,1},{6,2},{7,3},{8,4},{9,5},{1... | collective-permute-start | bytes 129032 | tf_op jit(solution)/shard_map/ppermute | solution.py:180
  43.2 6.0 %collective-permute-start.11 = (bf16[24,896]{1,0:T(8,128)(2,1)S(1)}, bf16[24,896]{1,0:T(8,128)(2,1)S(1)}, u32[]{:S(2)}, u32[]{:S(2)}) collective-permute-start(bf16[24,896]{1,0:T(8,128)(2,1)S(1)} %get-tuple-element.34), channel_id=1, source_target_pairs={{0,4},{1,5},{2,6},{3,7},{4,8},{5,9},{6,10},{7,11},{8,12},{9,13},{1... | collective-permute-start | bytes 129032 | tf_op jit(solution)/shard_map/ppermute | solution.py:180
  43.6 5.7 %collective-permute-start.10 = (bf16[24,896]{1,0:T(8,128)(2,1)S(1)}, bf16[24,896]{1,0:T(8,128)(2,1)S(1)}, u32[]{:S(2)}, u32[]{:S(2)}) collective-permute-start(bf16[24,896]{1,0:T(8,128)(2,1)S(1)} %get-tuple-element.35), channel_id=1, source_target_pairs={{0,8},{1,9},{2,10},{3,11},{4,12},{5,13},{6,14},{7,15},{8,0},{9,1},... | collective-permute-start | bytes 129032 | tf_op jit(solution)/shard_map/ppermute | solution.py:180
  45.5 5.1 %collective-permute-start.14 = (bf16[24,896]{1,0:T(8,128)(2,1)S(1)}, bf16[24,896]{1,0:T(8,128)(2,1)S(1)}, u32[]{:S(2)}, u32[]{:S(2)}) collective-permute-start(bf16[24,896]{1,0:T(8,128)(2,1)S(1)} %get-tuple-element.36), channel_id=1, source_target_pairs={{0,12},{1,13},{2,14},{3,15},{4,0},{5,1},{6,2},{7,3},{8,4},{9,5},{1... | collective-permute-start | bytes 129032 | tf_op jit(solution)/shard_map/ppermute | solution.py:180
  47.2 5.9 %collective-permute-start.16 = (bf16[24,896]{1,0:T(8,128)(2,1)S(1)}, bf16[24,896]{1,0:T(8,128)(2,1)S(1)}, u32[]{:S(2)}, u32[]{:S(2)}) collective-permute-start(bf16[24,896]{1,0:T(8,128)(2,1)S(1)} %get-tuple-element.37), channel_id=1, source_target_pairs={{0,4},{1,5},{2,6},{3,7},{4,8},{5,9},{6,10},{7,11},{8,12},{9,13},{1... | collective-permute-start | bytes 129032 | tf_op jit(solution)/shard_map/ppermute | solution.py:180
  47.8 5.4 %collective-permute-start.15 = (bf16[24,896]{1,0:T(8,128)(2,1)S(1)}, bf16[24,896]{1,0:T(8,128)(2,1)S(1)}, u32[]{:S(2)}, u32[]{:S(2)}) collective-permute-start(bf16[24,896]{1,0:T(8,128)(2,1)S(1)} %get-tuple-element.38), channel_id=1, source_target_pairs={{0,8},{1,9},{2,10},{3,11},{4,12},{5,13},{6,14},{7,15},{8,0},{9,1},... | collective-permute-start | bytes 129032 | tf_op jit(solution)/shard_map/ppermute | solution.py:180
